TPU v7x, 32 devices: a whole 2x2x4 slice. The times are simulated.
32 devices in a mesh: row: 4 (over z), col: 8 (over y, x, core).
Axes of the slice: x: 2, y: 2, z: 4, core: 2. Of those that a mesh axis runs over, the one named last changes fastest.
Arguments:
- inverse: float32 [16384, 16384], P('row', 'col'), may hold values from -0.0625 to 0.0625
- pattern: int32 [128, 128], P('row', 'col'), may hold values 0 or 1
- factor_first: float32 [16384, 256], P('col'), may hold values from -1.5 to 1.5
- factor_second: float32 [16384, 256], P('col'), may hold values from -1.5 to 1.5
- rows_first: int32 [64], replicated, may hold values from 0 to 127, as said below
- rows_second: int32 [64], replicated, may hold values from 0 to 127, as said below
- coupling: float32 [256, 256], replicated, may hold values from -0.375 to 0.375
- diag_first: float32 [256, 256], replicated, may hold values from -6 to 6
- diag_second: float32 [256, 256], replicated, may hold values from -6 to 6
Outputs:
- panel_one: float32 [16384, 256], P(('row', 'col'))
- panel_two: float32 [16384, 256], P(('row', 'col'))
- block_one: float32 [256, 256], replicated
- block_cross: float32 [256, 256], replicated
- block_two: float32 [256, 256], replicated
Inputs may be any that keep to these rules, and one draw needn't show every extreme that they name: `rows_first`: 64 distinct block indices in increasing order; the first block, the block 64 and the last block are always among them. `rows_second`: 64 distinct block indices in increasing order; the first block, the block 64 and the last block are always among them.
All inputs are finite; a program needn't handle non-finite values. No bound on the sum of `pattern` on one device may be relied on, other than what follows from the above.
Results may differ from a plain program's by a relative error of at most 0.000071.
Values sent between devices are 32-bit elements; how exact they have to be, the bound alone decides.
No kernel may reach another device: no remote copies, remote signals or barrier semaphores. Data moves between devices by JAX's collectives and lax.ppermute only.
A program may use at most 192 MiB of HBM per device.

v0:
```python
import jax
import jax.numpy as jnp
from jax import lax
from jax.sharding import PartitionSpec as P

BLK = 128


def member(block_ids, rows_list):
    hits = (block_ids[:, None] == rows_list[None, :]).astype(jnp.float32)
    return jnp.sum(hits, axis=1)


def per_device(
    inverse,
    pattern,
    factor_first,
    factor_second,
    rows_first,
    rows_second,
    coupling,
    diag_first,
    diag_second,
):
    high = lax.Precision.HIGHEST
    row_count = lax.axis_size("row")
    col_count = lax.axis_size("col")
    row_index = lax.axis_index("row")
    col_index = lax.axis_index("col")
    share_rows = factor_first.shape[0]
    panel_width = factor_first.shape[1]
    local_rows, local_cols = inverse.shape
    quota_rows = local_rows // col_count
    masked = (
        inverse.reshape(local_rows // BLK, BLK, local_cols // BLK, BLK)
        * pattern.astype(jnp.float32)[:, None, :, None]
    ).reshape(local_rows, local_cols)
    share_ids = (col_index * share_rows + jnp.arange(share_rows, dtype=jnp.int32)) // BLK
    own_start = (row_index * col_count + col_index) * quota_rows
    own_ids = (own_start + jnp.arange(quota_rows, dtype=jnp.int32)) // BLK

    def fetch_rows(factor):
        ratio_roots = col_count // row_count
        pieces = factor.reshape(row_count, quota_rows, panel_width)
        tiled = jnp.tile(pieces, (ratio_roots, 1, 1))
        owner_slot = col_index - row_index * ratio_roots
        slot_ids = jnp.arange(col_count, dtype=jnp.int32)
        keep_slot = jnp.logical_and(
            slot_ids // row_count == owner_slot, col_index // ratio_roots == row_index
        )
        outgoing = jnp.where(keep_slot[:, None, None], tiled, jnp.zeros_like(tiled)).reshape(
            col_count * quota_rows, panel_width
        )
        received = lax.all_to_all(outgoing, "col", split_axis=0, concat_axis=0, tiled=True)
        owner = row_index * ratio_roots + col_index // row_count
        return lax.dynamic_slice_in_dim(received, owner * quota_rows, quota_rows, 0)

    def panel_product(factor_kept):
        return lax.psum_scatter(
            jnp.dot(masked, factor_kept, precision=high), "col", scatter_dimension=0, tiled=True
        )

    x_one = factor_first * member(share_ids, rows_first)[:, None]
    x_two = factor_second * member(share_ids, rows_second)[:, None]
    panel_one = -panel_product(x_one)
    near_one = fetch_rows(factor_first)
    near_one = near_one * member(own_ids, rows_first)[:, None]
    first_total = lax.psum(jnp.dot(near_one.T, panel_one, precision=high), ("row", "col"))
    block_one = diag_first - first_total
    near_two = fetch_rows(factor_second)
    near_two = near_two * member(own_ids, rows_second)[:, None]
    panel_two = -(panel_product(x_two) + jnp.dot(panel_one, coupling, precision=high))
    cross_sum, quad_sum = lax.psum(
        (
            jnp.dot(panel_one.T, near_two, precision=high),
            jnp.dot(near_two.T, panel_two, precision=high),
        ),
        ("row", "col"),
    )
    block_cross = -(cross_sum + jnp.dot(block_one, coupling, precision=high))
    block_two = diag_second - quad_sum - jnp.dot(coupling.T, block_cross, precision=high)
    return (panel_one, panel_two, block_one, block_cross, block_two)


def solution(mesh):
    return jax.shard_map(
        per_device,
        mesh=mesh,
        in_specs=(
            P("row", "col"),
            P("row", "col"),
            P("col", None),
            P("col", None),
            P(),
            P(),
            P(),
            P(),
            P(),
        ),
        out_specs=(P(("row", "col"), None), P(("row", "col"), None), P(), P(), P()),
        check_vma=False,
    )
```

profile of v0, /device:TPU:0, one launch (start us, length us, event | category | flops | bytes accessed | tf_op | source)
XLA Modules:
  0.0 368.2 jit_solution(11985239225750703956)
XLA Ops:
  7.2 0.0 copy-start
  7.2 0.0 reduce-scatter.3.cloned.1.call-start
  7.2 0.7 convert_element_type.15
  8.0 0.1 copy.16
  8.1 0.9 convert_reduce_fusion
  8.9 0.0 copy-start.1
  8.9 11.2 %mul.62 = f32[32,128,16,128]{3,2,1,0:T(8,128)} broadcast(f32[32,16]{1,0:T(8,128)S(1)} %copy.16), dimensions={0,2} | broadcast | bytes 33556480 | tf_op jit(solution)/shard_map/mul | solution.py:35
  20.1 0.0 copy-done.1
  20.1 44.0 %fusion.1 = f32[4096,256]{1,0:T(8,128)} fusion(f32[4096,2048]{1,0:T(8,128)} %param.9, f32[512,8,16,128]{3,2,1,0:T(8,128)} %bitcast.27, f32[2048,256]{1,0:T(8,128)S(1)} %copy-done.1, f32[2048]{0:T(1024)S(1)} %get-tuple-element.6), kind=kOutput, calls=%fused_computation.2 | convolution fusion | flops 25778716672 | bytes 73408512 | tf_op jit(solution)/shard_map/dot_general | solution.py:60
  64.2 0.0 reduce-scatter.3.cloned.1.call-update
  64.3 6.0 %bitcast_select_fusion = (f32[8,512,256]{2,1,0:T(8,128)}, f32[8,512,256]{2,1,0:T(8,128)}) fusion(f32[4,512,256]{2,1,0:T(8,128)} %bitcast.30, pred[8]{0:T(512)(128)(4,1)S(1)} %compare_and_fusion, f32[4,512,256]{2,1,0:T(8,128)S(1)} %bitcast.29), kind=kLoop, calls=%fused_computation.3 | loop fusion | flops 2097152 | bytes 12582920 | tf_op jit(solution)/shard_map/jit(_where)/select_n | solution.py:51
  70.3 5.4 %all-to-all-start.1 = ((f32[8,512,256]{2,1,0:T(8,128)}), f32[8,512,256]{2,1,0:T(8,128)}, u32[]{:S(2)}, u32[]{:S(2)}) async-start(f32[8,512,256]{2,1,0:T(8,128)} %get-tuple-element.12), calls=%async_computation.3 | async-start | bytes 8388608 | tf_op jit(solution)/shard_map/all_to_all | solution.py:54
  75.7 0.2 reduce-scatter.5.cloned.1.call-start
  75.9 0.0 copy-done.2
  76.0 45.2 %fusion = f32[4096,256]{1,0:T(8,128)} fusion(f32[4096,2048]{1,0:T(8,128)} %param.9, f32[512,8,16,128]{3,2,1,0:T(8,128)} %bitcast.28, f32[2048,256]{1,0:T(8,128)S(1)} %copy-done.2, f32[2048]{0:T(1024)S(1)} %get-tuple-element.5), kind=kOutput, calls=%fused_computation.1 | convolution fusion | flops 25778716672 | bytes 73408512 | tf_op jit(solution)/shard_map/dot_general | solution.py:60
  121.1 0.0 reduce-scatter.5.cloned.1.call-update
  121.2 16.3 %all-to-all-done.1 = f32[8,512,256]{2,1,0:T(8,128)} async-done(((f32[8,512,256]{2,1,0:T(8,128)}), f32[8,512,256]{2,1,0:T(8,128)}, u32[]{:S(2)}, u32[]{:S(2)}) %all-to-all-start.1) | async-done | bytes 4194336 | tf_op jit(solution)/shard_map/all_to_all | solution.py:54
  137.5 4.7 %all-to-all-start = ((f32[8,512,256]{2,1,0:T(8,128)}), f32[8,512,256]{2,1,0:T(8,128)}, u32[]{:S(2)}, u32[]{:S(2)}) async-start(f32[8,512,256]{2,1,0:T(8,128)} %get-tuple-element.13), calls=%async_computation.2 | async-start | bytes 8388608 | tf_op jit(solution)/shard_map/all_to_all | solution.py:54
  142.2 0.0 copy-start.7
  142.2 0.3 all-reduce.3.cloned.1.call-start
  142.5 0.0 copy-done.9
  142.5 0.0 copy-done.10
  142.5 0.1 convert_reduce_fusion.2
  142.6 0.2 reduce-scatter.3.cloned.1.call-done
  142.8 1.1 neg.9
  143.9 0.0 copy-start.3
  143.9 0.0 copy-start.8
  143.9 3.0 fusion.13
  147.0 72.0 %reduce-scatter.5.cloned.1.call-done = f32[512,256]{1,0:T(8,128)} async-done(((f32[4096,256]{1,0:T(8,128)}), f32[512,256]{1,0:T(8,128)}) %reduce-scatter.5.cloned.1.call-update) | async-done | bytes 524304 | tf_op jit(solution)/shard_map/reduce_scatter | solution.py:59
  219.0 0.0 copy-done
  219.0 1.6 fusion.4
  220.6 0.0 copy-start.4
  220.6 3.0 fusion.12
  223.7 0.0 all-to-all-done
  223.7 2.8 fusion.9
  226.5 0.0 all-reduce.3.cloned.1.call-update
  226.5 130.3 %all-reduce.3.cloned.1.call-done = (f32[256,256]{1,0:T(8,128)}, f32[256,256]{1,0:T(8,128)}, f32[256,256]{1,0:T(8,128)}) async-done(((f32[256,256]{1,0:T(8,128)}, f32[256,256]{1,0:T(8,128)}, f32[256,256]{1,0:T(8,128)}), (f32[256,256]{1,0:T(8,128)}, f32[256,256]{1,0:T(8,128)}, f32[256,256]{1,0:T(8,128)})) %all-reduce.3.cloned.1.call-update) | async-done | bytes 786448 | tf_op jit(solution)/shard_map/psum | solution.py:68
  356.9 0.0 copy-done.7
  356.9 1.0 sub.45
  357.8 0.0 copy-start.5
  357.9 1.4 fusion.6
  359.3 0.0 copy-done.3
  359.3 0.0 copy-start.6
  359.3 0.0 copy-done.8
  359.3 2.3 fusion.5
  361.7 0.0 copy-done.4
  361.7 0.0 copy-done.5
  361.7 0.0 copy-done.6
  (6 shorter events, 0.0 us)
Async XLA Ops:
  7.2 211.8 %copy-start = (f32[256,256]{1,0:T(8,128)S(1)}, f32[256,256]{1,0:T(8,128)}, u32[]{:S(2)}) copy-start(f32[256,256]{1,0:T(8,128)} %param.15) | copy-start | bytes 786436
  7.2 135.6 %reduce-scatter.3.cloned.1.call-start = ((), (), s32[]{:S(2)}) async-start(), calls=%async_computation.4 | async-start | bytes 4718592 | tf_op jit(solution)/shard_map/reduce_scatter | solution.py:59
  8.9 11.2 %copy-start.1 = (f32[2048,256]{1,0:T(8,128)S(1)}, f32[2048,256]{1,0:T(8,128)}, u32[]{:S(2)}) copy-start(f32[2048,256]{1,0:T(8,128)} %param.11) | copy-start | bytes 6291460
  70.3 5.7 %copy-start.2 = (f32[2048,256]{1,0:T(8,128)S(1)}, f32[2048,256]{1,0:T(8,128)}, u32[]{:S(2)}) copy-start(f32[2048,256]{1,0:T(8,128)} %param.12) | copy-start | bytes 6291460
  70.3 67.2 %all-to-all-start.1 = ((f32[8,512,256]{2,1,0:T(8,128)}), f32[8,512,256]{2,1,0:T(8,128)}, u32[]{:S(2)}, u32[]{:S(2)}) async-start(f32[8,512,256]{2,1,0:T(8,128)} %get-tuple-element.12), calls=%async_computation.3 | async-start | bytes 8388608 | tf_op jit(solution)/shard_map/all_to_all | solution.py:54
  75.7 143.2 %reduce-scatter.5.cloned.1.call-start = ((), (), s32[]{:S(2)}) async-start(), calls=%async_computation.5 | async-start | bytes 4718592 | tf_op jit(solution)/shard_map/reduce_scatter | solution.py:59
  137.5 5.0 %copy-start.9 = (s32[64]{0:T(128)S(1)}, s32[64]{0:T(128)}, u32[]{:S(2)}) copy-start(s32[64]{0:T(128)} %param.14) | copy-start | bytes 772
  137.5 5.0 %copy-start.10 = (s32[64]{0:T(128)S(1)}, s32[64]{0:T(128)}, u32[]{:S(2)}) copy-start(s32[64]{0:T(128)} %param.13) | copy-start | bytes 772
  137.5 86.2 %all-to-all-start = ((f32[8,512,256]{2,1,0:T(8,128)}), f32[8,512,256]{2,1,0:T(8,128)}, u32[]{:S(2)}, u32[]{:S(2)}) async-start(f32[8,512,256]{2,1,0:T(8,128)} %get-tuple-element.13), calls=%async_computation.2 | async-start | bytes 8388608 | tf_op jit(solution)/shard_map/all_to_all | solution.py:54
  142.2 214.7 %copy-start.7 = (f32[256,256]{1,0:T(8,128)S(1)}, f32[256,256]{1,0:T(8,128)}, u32[]{:S(2)}) copy-start(f32[256,256]{1,0:T(8,128)} %param.16) | copy-start | bytes 786436
  142.2 214.6 %all-reduce.3.cloned.1.call-start = ((), (), s32[]{:S(2)}) async-start(), calls=%async_computation.6 | async-start | bytes 1572864 | tf_op jit(solution)/shard_map/psum | solution.py:68
  143.9 215.4 %copy-start.3 = (f32[512,256]{1,0:T(8,128)}, f32[512,256]{1,0:T(8,128)S(1)}, u32[]{:S(2)}) copy-start(f32[512,256]{1,0:T(8,128)S(1)} %neg.9) | copy-start | bytes 1572868
  143.9 215.4 %copy-start.8 = (f32[256,256]{1,0:T(8,128)S(1)}, f32[256,256]{1,0:T(8,128)}, u32[]{:S(2)}) copy-start(f32[256,256]{1,0:T(8,128)} %param.17) | copy-start | bytes 786436
  220.6 141.1 %copy-start.4 = (f32[512,256]{1,0:T(8,128)}, f32[512,256]{1,0:T(8,128)S(1)}, u32[]{:S(2)}) copy-start(f32[512,256]{1,0:T(8,128)S(1)} %fusion.4) | copy-start | bytes 1572868
  357.8 3.8 %copy-start.5 = (f32[256,256]{1,0:T(8,128)}, f32[256,256]{1,0:T(8,128)S(1)}, u32[]{:S(2)}) copy-start(f32[256,256]{1,0:T(8,128)S(1)} %sub.45) | copy-start | bytes 786436
  359.3 2.4 copy-start.6
Sparse Core Ops, SparseCore 0:
  64.3 78.4 reduce-scatter.2
  146.6 72.3 reduce-scatter.4
  226.6 130.1 all-reduce.2
where the time goes:
time: 369 us; the launch traced here: 368 us
  waiting for transfers between devices  219 us (59%)
  matrix products  104 us (28%)
  between operations  14 us (4%)
  local copies, waits for them, and re-layouts  11.3 us (3%)
  starting transfers between devices  10.7 us (3%)
  other arithmetic  9.84 us (3%)
    psum x1, waiting for transfers between devices, per_device(): lax.psum(jnp.dot(near_one.T, panel_one, precision=high), ('row', 'col'))  130 us
    dot_general x2, matrix products, panel_product(): jnp.dot(masked, factor_kept, precision=high)  89.2 us
    reduce_scatter x2, waiting for transfers between devices, panel_product(): lax.psum_scatter(jnp.dot(masked, factor_kept, precision=high), 'col', sca...  72.2 us
    all_to_all x2, waiting for transfers between devices, fetch_rows(): lax.all_to_all(outgoing, 'col', split_axis=0, concat_axis=0, tiled=True)  16.3 us
    mul x1, local copies, waits for them, and re-layouts, per_device(): inverse.reshape(local_rows // BLK, BLK, local_cols // BLK, BLK)  11.2 us
    all_to_all x2, starting transfers between devices, fetch_rows(): lax.all_to_all(outgoing, 'col', split_axis=0, concat_axis=0, tiled=True)  10.1 us
  transfers between devices with their start and end apart: 5, of which 4 were waited for; matrix products, arithmetic and copies ran while one was open for 16% of the time, Pallas kernels for 0%

commit v1 on v0

v1 whole, which is shorter than its diff:
```python
import functools

import jax
import jax.numpy as jnp
from jax import lax
from jax.experimental import pallas as pl
from jax.experimental.pallas import tpu as pltpu
from jax.sharding import PartitionSpec as P

BLK = 128
AXES = ("row", "col")
F32 = jnp.float32
BF16 = jnp.bfloat16
VMEM_LIMIT = 48 * 1024 * 1024


def halves(value):
    high = value.astype(BF16)
    low = (value - high.astype(F32)).astype(BF16)
    return high, low


def dot3(a, b, dims=(((1,), (0,)), ((), ()))):
    a_high, a_low = halves(a)
    b_high, b_low = halves(b)
    mul = functools.partial(lax.dot_general, dimension_numbers=dims, preferred_element_type=F32)
    return mul(a_high, b_high) + (mul(a_high, b_low) + mul(a_low, b_high))


ROWS_DIM = (((0,), (0,)), ((), ()))


def member(block_ids, rows_list):
    hits = (block_ids[:, None] == rows_list[None, :]).astype(F32)
    return jnp.sum(hits, axis=1)


def prepare_body(first_ref, second_ref, keep_ref, high_ref, low_ref):
    width = first_ref.shape[1]
    for at, ref in enumerate((first_ref, second_ref)):
        high, low = halves(ref[...] * keep_ref[:, at : at + 1])
        high_ref[:, at * width : (at + 1) * width] = high
        low_ref[:, at * width : (at + 1) * width] = low


def prepare(first, second, keep):
    rows, width = first.shape
    tile = min(rows, 512)
    spec = lambda cols: pl.BlockSpec((tile, cols), lambda i: (i, 0))
    return pl.pallas_call(
        prepare_body,
        grid=(rows // tile,),
        in_specs=[spec(width), spec(width), spec(2)],
        out_specs=[spec(2 * width)] * 2,
        out_shape=[jax.ShapeDtypeStruct((rows, 2 * width), BF16)] * 2,
        compiler_params=pltpu.CompilerParams(vmem_limit_bytes=VMEM_LIMIT),
        name="prepare",
    )(first, second, keep)


def product_body(at_ref, a_ref, mask_ref, high_ref, low_ref, *rest):
    out_ref = rest[-1]
    tile, depth = a_ref.shape
    block0 = at_ref[0] * (tile // BLK) + pl.program_id(0) * (tile // BLK)
    parts = []
    for block in range(tile // BLK):
        mask = mask_ref[pl.ds(block0 + block, 1), :]
        parts.append(a_ref[block * BLK : (block + 1) * BLK, :] * mask)
    a = jnp.concatenate(parts, axis=0) if len(parts) > 1 else parts[0]
    a_high, a_low = halves(a)
    mul = functools.partial(jnp.dot, preferred_element_type=F32)
    out = mul(a_high, high_ref[...]) + mul(a_high, low_ref[...]) + mul(a_low, high_ref[...])
    if len(rest) > 1:
        out = out + rest[0][...]
    out_ref[...] = out


def product(inverse, mask, high, low, piece, piece_rows, add=None, tile=256):
    depth, width = high.shape
    tile = min(tile, piece_rows)
    steps = piece_rows // tile
    whole = lambda shape: pl.BlockSpec(shape, lambda i, at: (0, 0), pipeline_mode=pl.Buffered(1))
    out_spec = pl.BlockSpec((tile, width), lambda i, at: (i, 0))
    extra = [] if add is None else [add]
    return pl.pallas_call(
        product_body,
        grid_spec=pltpu.PrefetchScalarGridSpec(
            num_scalar_prefetch=1,
            grid=(steps,),
            in_specs=[
                pl.BlockSpec((tile, depth), lambda i, at: (at[0] + i, 0)),
                whole(mask.shape),
                whole(high.shape),
                whole(low.shape),
            ]
            + [out_spec] * len(extra),
            out_specs=out_spec,
        ),
        out_shape=jax.ShapeDtypeStruct((piece_rows, width), F32),
        compiler_params=pltpu.CompilerParams(vmem_limit_bytes=VMEM_LIMIT),
        cost_estimate=pl.CostEstimate(
            flops=6 * piece_rows * depth * width,
            bytes_accessed=4 * piece_rows * (depth + width),
            transcendentals=0,
        ),
        name="product",
    )((piece * steps).astype(jnp.int32).reshape(1), inverse, mask, high, low, *extra)


def finish_body(near_ref, keep_ref, coupling_ref, own_ref, *rest):
    *added, one_ref, two_ref, sums_ref = rest
    total = own_ref[...]
    for ref in added:
        total = total + ref[...]
    width = coupling_ref.shape[0]
    x_one = near_ref[0] * keep_ref[:, 0:1]
    x_two = near_ref[1] * keep_ref[:, 1:2]
    one = -total[:, :width]
    two = -(total[:, width:] + dot3(one, coupling_ref[...]))
    one_ref[...] = one
    two_ref[...] = two
    sums_ref[:width] = dot3(x_one, one, ROWS_DIM)
    sums_ref[width : 2 * width] = dot3(one, x_two, ROWS_DIM)
    sums_ref[2 * width :] = dot3(x_two, two, ROWS_DIM)


def finish(near, keep, coupling, own, added):
    rows = own.shape[0]
    width = coupling.shape[0]
    return pl.pallas_call(
        finish_body,
        out_shape=[
            jax.ShapeDtypeStruct((rows, width), F32),
            jax.ShapeDtypeStruct((rows, width), F32),
            jax.ShapeDtypeStruct((3 * width, width), F32),
        ],
        compiler_params=pltpu.CompilerParams(vmem_limit_bytes=VMEM_LIMIT),
        name="finish",
    )(near, keep, coupling, own, *added)


def close_body(sums_ref, coupling_ref, first_ref, second_ref, one_ref, cross_ref, two_ref):
    width = coupling_ref.shape[0]
    coupling = coupling_ref[...]
    one = first_ref[...] - sums_ref[:width]
    cross = -(sums_ref[width : 2 * width] + dot3(one, coupling))
    one_ref[...] = one
    cross_ref[...] = cross
    two_ref[...] = second_ref[...] - sums_ref[2 * width :] - dot3(coupling, cross, ROWS_DIM)


def close(sums, coupling, diag_first, diag_second):
    return pl.pallas_call(
        close_body,
        out_shape=[jax.ShapeDtypeStruct(coupling.shape, F32)] * 3,
        compiler_params=pltpu.CompilerParams(vmem_limit_bytes=VMEM_LIMIT),
        name="close",
    )(sums, coupling, diag_first, diag_second)


def flip(value, count, mask_of):
    return lax.ppermute(value, AXES, [(i, i ^ mask_of(i)) for i in range(count)])


def bits_of(count):
    return count.bit_length() - 1


def total_over_all(value, rows, cols, me):
    count = rows * cols
    order = [1 << bit for bit in range(bits_of(count))]
    for bit in order:
        half = value.shape[0] // 2
        mine = ((me & bit) != 0).astype(jnp.int32)
        sent = lax.dynamic_slice_in_dim(value, (1 - mine) * half, half, 0)
        kept = lax.dynamic_slice_in_dim(value, mine * half, half, 0)
        value = kept + flip(sent, count, lambda i: bit)
    for bit in reversed(order):
        other = flip(value, count, lambda i: bit)
        low = (me & bit) == 0
        value = jnp.concatenate(
            [jnp.where(low, value, other), jnp.where(low, other, value)], axis=0
        )
    return value


def per_device(
    inverse,
    pattern,
    factor_first,
    factor_second,
    rows_first,
    rows_second,
    coupling,
    diag_first,
    diag_second,
):
    row_count = lax.axis_size("row")
    col_count = lax.axis_size("col")
    count = row_count * col_count
    row_index = lax.axis_index("row")
    col_index = lax.axis_index("col")
    me = row_index * col_count + col_index
    share_rows = factor_first.shape[0]
    local_rows, local_cols = inverse.shape
    quota_rows = local_rows // col_count

    piece_at = row_index ^ (col_index & (row_count - 1))
    outgoing = jnp.stack(
        [
            lax.dynamic_slice_in_dim(factor, piece_at * quota_rows, quota_rows, 0)
            for factor in (factor_first, factor_second)
        ]
    )
    moves = []
    for k in range(row_count):
        for c in range(col_count):
            moves.append((k * col_count + c, c * row_count + (k ^ (c & (row_count - 1)))))
    near = lax.ppermute(outgoing, AXES, moves)

    def keep_of(start, rows):
        ids = (start + jnp.arange(rows, dtype=jnp.int32)) // BLK
        return jnp.stack([member(ids, rows_first), member(ids, rows_second)], axis=1)

    keep = keep_of(col_index * share_rows, share_rows)
    near_keep = keep_of(me * quota_rows, quota_rows)
    mask = jnp.repeat(pattern.astype(F32), BLK, axis=1)
    high, low = prepare(factor_first, factor_second, keep)

    core = col_index & 1
    spare = bits_of(col_count) - 1
    forward = [2 << bit for bit in range(spare)]
    backward = list(reversed(forward))
    arrived = {e: [] for e in range(1 << spare)}
    order = sorted(arrived, key=lambda e: -int(format(e, "b").zfill(spare)[::-1] or "0", 2))
    own = None
    for e in order:
        offsets = [
            sum(bit for at, bit in enumerate(line) if e >> at & 1) for line in (forward, backward)
        ]
        mine = col_index ^ jnp.where(core == 0, offsets[0], offsets[1])
        theirs = col_index ^ 1 ^ jnp.where(core == 1, offsets[0], offsets[1])
        partner = product(inverse, mask, high, low, theirs, quota_rows)
        partner = flip(partner, count, lambda i: 1)
        total = product(inverse, mask, high, low, mine, quota_rows)
        total = total + partner
        for part in arrived[e]:
            total = total + part
        if e:
            at = (e & -e).bit_length() - 1
            got = flip(total, count, lambda i: (backward if i & 1 else forward)[at])
            arrived[e & (e - 1)].append(got)
        else:
            own = total
    panel_one, panel_two, sums = finish(near, near_keep, coupling, own, [])
    sums = total_over_all(sums, row_count, col_count, me)
    block_one, block_cross, block_two = close(sums, coupling, diag_first, diag_second)
    return (panel_one, panel_two, block_one, block_cross, block_two)


def solution(mesh):
    return jax.shard_map(
        per_device,
        mesh=mesh,
        in_specs=(
            P("row", "col"),
            P("row", "col"),
            P("col", None),
            P("col", None),
            P(),
            P(),
            P(),
            P(),
            P(),
        ),
        out_specs=(P(AXES, None), P(AXES, None), P(), P(), P()),
        check_vma=False,
    )
```

time: 369 us -> 192 us (0.52)
  waiting for transfers between devices: 219 us -> 74.9 us
  matrix products: 104 us -> 0 us
  Pallas kernels: 0 us -> 51.9 us
  starting transfers between devices: 10.7 us -> 37.9 us
  between operations: 14 us -> 1.03 us
    psum x1 -> x0, waiting for transfers between devices: 130 us -> none  [per_device(): lax.psum(jnp.dot(near_one.T, panel_one, precision=high), ('row', 'col'))]
    dot_general x8 -> x0, matrix products: 104 us -> none  [the longest x2 89.2 us: panel_product(): jnp.dot(masked, factor_kept, precision=high)]
    ppermute x0 -> x18, waiting for transfers between devices: none -> 74.9 us  [the longest x17 74.9 us: flip(): lax.ppermute(value, AXES, [(i, i ^ mask_of(i)) for i in range(count)])]
    reduce_scatter x2 -> x0, waiting for transfers between devices: 72.2 us -> none  [panel_product(): lax.psum_scatter(jnp.dot(masked, factor_kept, precision=high), 'col', sca...]
    pallas_call x0 -> x11, Pallas kernels: none -> 51.9 us  [the longest x8 44.6 us: product(): pl.pallas_call(product_body, grid_spec=pltpu.PrefetchScalarGridSpec(num_s...]
    ppermute x0 -> x18, starting transfers between devices: none -> 37.9 us  [the longest x17 28.5 us: flip(): lax.ppermute(value, AXES, [(i, i ^ mask_of(i)) for i in range(count)])]
    all_to_all x2 -> x0, waiting for transfers between devices: 16.3 us -> none  [fetch_rows(): lax.all_to_all(outgoing, 'col', split_axis=0, concat_axis=0, tiled=True)]
    mul x1 -> x0, local copies, waits for them, and re-layouts: 11.2 us -> none  [per_device(): inverse.reshape(local_rows // BLK, BLK, local_cols // BLK, BLK)]
  transfers between devices with their start and end apart: 5 -> 18, of which waited for: 4 -> 11; matrix products, arithmetic and copies ran while one was open for 16% -> 7% of each run, Pallas kernels for 0% -> 20%
where the time goes in v1:
time: 192 us; the launch traced here: 191 us
  waiting for transfers between devices  74.9 us (39%)
  Pallas kernels  51.9 us (27%)
  starting transfers between devices  37.9 us (20%)
  other arithmetic  13.2 us (7%)
  local copies, waits for them, and re-layouts  11.8 us (6%)
    ppermute x17, waiting for transfers between devices, flip(): lax.ppermute(value, AXES, [(i, i ^ mask_of(i)) for i in range(count)])  74.9 us
    pallas_call x8, Pallas kernels, product(): pl.pallas_call(product_body, grid_spec=pltpu.PrefetchScalarGridSpec(num_s...  44.6 us
    ppermute x17, starting transfers between devices, flip(): lax.ppermute(value, AXES, [(i, i ^ mask_of(i)) for i in range(count)])  28.5 us
    unnamed x25, local copies, waits for them, and re-layouts  9.65 us
    ppermute x1, starting transfers between devices, per_device(): near = lax.ppermute(outgoing, AXES, moves)  9.45 us
    add x2, other arithmetic, per_device(): total = total + part  5.28 us
    add x2, other arithmetic, per_device(): total = total + partner  4.87 us
  transfers between devices with their start and end apart: 18, of which 11 were waited for; matrix products, arithmetic and copies ran while one was open for 7% of the time, Pallas kernels for 20%

profile of v1, /device:TPU:0, one launch (start us, length us, event | category | flops | bytes accessed | tf_op | source)
XLA Modules:
  0.0 190.7 jit_solution(4214689002864374239)
XLA Ops:
  0.7 0.9 convert_reduce_fusion.1
  1.9 0.7 convert_element_type.32
  2.9 3.3 %prepare.1 = (bf16[2048,512]{1,0:T(8,128)(2,1)S(1)}, bf16[2048,512]{1,0:T(8,128)(2,1)S(1)}) custom-call(f32[2048,256]{1,0:T(8,128)} %first_ref.2, f32[2048,256]{1,0:T(8,128)} %second_ref.2, f32[2048,2]{1,0:T(8,128)S(1)} %copy.24.keep_ref), custom_call_target="tpu_custom_call" | custom-call | tf_op jit(solution)/shard_map/prepare/pallas_call | solution.py:50
  6.3 6.7 %product.15 = f32[512,512]{1,0:T(8,128)} custom-call(s32[1]{0:T(128)} %bitcast.13.at_ref, f32[4096,2048]{1,0:T(8,128)} %a_ref.15, f32[32,2048]{1,0:T(8,128)S(1)} %bitcast.20, bf16[2048,512]{1,0:T(8,128)(2,1)S(1)} %get-tuple-element.13.high_ref, bf16[2048,512]{1,0:T(8,128)(2,1)S(1)} %get-tuple-element.14.low_ref), custom_call_target="tpu_custom_call" | custom-call | flops 3221225472 | bytes 5242880 | tf_op jit(solution)/shard_map/product/pallas_call | solution.py:85
  13.0 0.5 collective-permute-start.5
  13.5 1.6 copy-done.1
  15.1 5.2 %product.13 = f32[512,512]{1,0:T(8,128)S(1)} custom-call(s32[1]{0:T(128)} %bitcast.11.at_ref, f32[4096,2048]{1,0:T(8,128)} %a_ref.15, f32[32,2048]{1,0:T(8,128)S(1)} %bitcast.21, bf16[2048,512]{1,0:T(8,128)(2,1)S(1)} %get-tuple-element.13.high_ref, bf16[2048,512]{1,0:T(8,128)(2,1)S(1)} %copy-done.1), custom_call_target="tpu_custom_call" | custom-call | flops 3221225472 | bytes 5242880 | tf_op jit(solution)/shard_map/product/pallas_call | solution.py:85
  20.4 1.6 copy-done.2
  22.0 6.0 %product.11 = f32[512,512]{1,0:T(8,128)} custom-call(s32[1]{0:T(128)} %bitcast.9.at_ref, f32[4096,2048]{1,0:T(8,128)} %a_ref.15, f32[32,2048]{1,0:T(8,128)S(1)} %bitcast.22, bf16[2048,512]{1,0:T(8,128)(2,1)S(1)} %get-tuple-element.13.high_ref, bf16[2048,512]{1,0:T(8,128)(2,1)S(1)} %copy-done.2), custom_call_target="tpu_custom_call" | custom-call | flops 3221225472 | bytes 5242880 | tf_op jit(solution)/shard_map/product/pallas_call | solution.py:85
  27.9 0.5 collective-permute-start.2
  28.4 1.6 copy-done.3
  30.0 5.2 %product.14 = f32[512,512]{1,0:T(8,128)S(1)} custom-call(s32[1]{0:T(128)} %bitcast.12.at_ref, f32[4096,2048]{1,0:T(8,128)} %a_ref.15, f32[32,2048]{1,0:T(8,128)S(1)} %bitcast.23, bf16[2048,512]{1,0:T(8,128)(2,1)S(1)} %get-tuple-element.13.high_ref, bf16[2048,512]{1,0:T(8,128)(2,1)S(1)} %copy-done.3), custom_call_target="tpu_custom_call" | custom-call | flops 3221225472 | bytes 5242880 | tf_op jit(solution)/shard_map/product/pallas_call | solution.py:85
  35.2 2.5 %add.103 = f32[512,512]{1,0:T(8,128)} add(f32[512,512]{1,0:T(8,128)S(1)} %product.14, f32[512,512]{1,0:T(8,128)} %collective-permute-done.5) | non-fusion elementwise | flops 262144 | bytes 3145728 | tf_op jit(solution)/shard_map/add | solution.py:246
  37.7 2.5 %collective-permute-start.6 = (f32[512,512]{1,0:T(8,128)}, f32[512,512]{1,0:T(8,128)}, u32[]{:S(2)}, u32[]{:S(2)}) collective-permute-start(f32[512,512]{1,0:T(8,128)} %add.103), channel_id=1, source_target_pairs={{0,2},{1,5},{2,0},{3,7},{4,6},{5,1},{6,4},{7,3},{8,10},{9,13},{10,... | collective-permute-start | bytes 3145736 | tf_op jit(solution)/shard_map/ppermute | solution.py:162
  40.2 1.6 copy-done.4
  41.8 6.0 %product.9 = f32[512,512]{1,0:T(8,128)} custom-call(s32[1]{0:T(128)} %bitcast.7.at_ref, f32[4096,2048]{1,0:T(8,128)} %a_ref.15, f32[32,2048]{1,0:T(8,128)S(1)} %bitcast.24, bf16[2048,512]{1,0:T(8,128)(2,1)S(1)} %get-tuple-element.13.high_ref, bf16[2048,512]{1,0:T(8,128)(2,1)S(1)} %copy-done.4), custom_call_target="tpu_custom_call" | custom-call | flops 3221225472 | bytes 5242880 | tf_op jit(solution)/shard_map/product/pallas_call | solution.py:85
  48.0 1.6 copy-done.5
  49.6 5.2 %product.12 = f32[512,512]{1,0:T(8,128)S(1)} custom-call(s32[1]{0:T(128)} %bitcast.10.at_ref, f32[4096,2048]{1,0:T(8,128)} %a_ref.15, f32[32,2048]{1,0:T(8,128)S(1)} %bitcast.25, bf16[2048,512]{1,0:T(8,128)(2,1)S(1)} %get-tuple-element.13.high_ref, bf16[2048,512]{1,0:T(8,128)(2,1)S(1)} %copy-done.5), custom_call_target="tpu_custom_call" | custom-call | flops 3221225472 | bytes 5242880 | tf_op jit(solution)/shard_map/product/pallas_call | solution.py:85
  54.8 5.2 %product.10 = f32[512,512]{1,0:T(8,128)S(1)} custom-call(s32[1]{0:T(128)} %bitcast.8.at_ref, f32[4096,2048]{1,0:T(8,128)} %a_ref.15, f32[32,2048]{1,0:T(8,128)S(1)} %bitcast.26, bf16[2048,512]{1,0:T(8,128)(2,1)S(1)} %get-tuple-element.13.high_ref, bf16[2048,512]{1,0:T(8,128)(2,1)S(1)} %copy-done.5), custom_call_target="tpu_custom_call" | custom-call | flops 3221225472 | bytes 5242880 | tf_op jit(solution)/shard_map/product/pallas_call | solution.py:85
  60.0 2.4 %add.100 = f32[512,512]{1,0:T(8,128)} add(f32[512,512]{1,0:T(8,128)S(1)} %product.10, f32[512,512]{1,0:T(8,128)} %collective-permute-done.2) | non-fusion elementwise | flops 262144 | bytes 3145728 | tf_op jit(solution)/shard_map/add | solution.py:246
  62.4 1.5 collective-permute-start.3
  63.9 2.9 %add_add_fusion = f32[512,512]{1,0:T(8,128)} fusion(f32[512,512]{1,0:T(8,128)} %collective-permute-done.6, f32[512,512]{1,0:T(8,128)S(1)} %product.12, f32[512,512]{1,0:T(8,128)} %collective-permute-done.4), kind=kLoop, calls=%fused_computation.1 | loop fusion | flops 524288 | bytes 4194304 | tf_op jit(solution)/shard_map/add | solution.py:248
  66.8 0.5 collective-permute-start.7
  67.3 1.3 dynamic-slice_bitcast_fusion
  68.6 1.0 pad_maximum_fusion
  69.6 9.5 %collective-permute-start = (f32[2,512,256]{2,1,0:T(8,128)}, f32[2,512,256]{2,1,0:T(8,128)}, u32[]{:S(2)}, u32[]{:S(2)}) collective-permute-start(f32[2,512,256]{2,1,0:T(8,128)} %pad_maximum_fusion), channel_id=1, source_target_pairs={{0,0},{1,5},{2,10},{3,15},{4,16},{5,21},{6,26},{7,31},{8,1},{9,4},... | collective-permute-start | bytes 3145736 | tf_op jit(solution)/shard_map/ppermute | solution.py:219
  79.4 1.6 copy-done.6
  81.0 5.2 %product.8 = f32[512,512]{1,0:T(8,128)S(1)} custom-call(s32[1]{0:T(128)} %bitcast.4.at_ref, f32[4096,2048]{1,0:T(8,128)} %a_ref.15, f32[32,2048]{1,0:T(8,128)S(1)} %bitcast.27, bf16[2048,512]{1,0:T(8,128)(2,1)S(1)} %get-tuple-element.13.high_ref, bf16[2048,512]{1,0:T(8,128)(2,1)S(1)} %copy-done.6), custom_call_target="tpu_custom_call" | custom-call | flops 3221225472 | bytes 5242880 | tf_op jit(solution)/shard_map/product/pallas_call | solution.py:85
  86.2 43.8 %collective-permute-done.3 = f32[512,512]{1,0:T(8,128)} collective-permute-done((f32[512,512]{1,0:T(8,128)}, f32[512,512]{1,0:T(8,128)}, u32[]{:S(2)}, u32[]{:S(2)}) %collective-permute-start.3) | collective-permute-done | bytes 1048608 | tf_op jit(solution)/shard_map/ppermute | solution.py:162
  130.1 2.3 %add_add_fusion.1.own_ref = f32[512,512]{1,0:T(8,128)S(1)} fusion(f32[512,512]{1,0:T(8,128)} %collective-permute-done.7, f32[512,512]{1,0:T(8,128)} %collective-permute-done.3, f32[512,512]{1,0:T(8,128)S(1)} %product.8, f32[512,512]{1,0:T(8,128)} %collective-permute-done.1), kind=kLoop, calls=%fused_computation.2 | loop fusion | flops 786432 | bytes 5242880 | tf_op jit(solution)/shard_map/add | solution.py:248
  132.4 2.6 %finish.1 = (f32[512,256]{1,0:T(8,128)}, f32[512,256]{1,0:T(8,128)}, f32[768,256]{1,0:T(8,128)S(1)}) custom-call(f32[2,512,256]{2,1,0:T(8,128)} %collective-permute-done.near_ref, f32[512,2]{1,0:T(8,128)S(1)} %copy.25.keep_ref, f32[256,256]{1,0:T(8,128)S(1)} %copy-done.7, f32[512,512]{1,0:T(8,128)S(1)} %add_add_fusion.1.own_ref), custom_call_target="tpu_custom_call" | custom-call | tf_op jit(solution)/shard_map/finish/pallas_call | solution.py:130
  135.1 9.0 %collective-permute-start.8 = (f32[384,256]{1,0:T(8,128)S(1)}, f32[384,256]{1,0:T(8,128)S(1)}, u32[]{:S(2)}, u32[]{:S(2)}) collective-permute-start(f32[384,256]{1,0:T(8,128)S(1)} %constant_dynamic-slice_fusion.4), channel_id=1, source_target_pairs={{0,1},{1,0},{2,3},{3,2},{4,5},{5,4},{6,7},{7,6},{8,9},{9,8},{10,11... | collective-permute-start | bytes 1179656 | tf_op jit(solution)/shard_map/ppermute | solution.py:162
  144.1 1.3 collective-permute-done.8
  145.6 7.2 %collective-permute-done.9 = f32[192,256]{1,0:T(8,128)S(1)} collective-permute-done((f32[192,256]{1,0:T(8,128)S(1)}, f32[192,256]{1,0:T(8,128)S(1)}, u32[]{:S(2)}, u32[]{:S(2)}) %collective-permute-start.9) | collective-permute-done | bytes 196640 | tf_op jit(solution)/shard_map/ppermute | solution.py:162
  152.8 2.6 %collective-permute-start.10 = (f32[96,256]{1,0:T(8,128)S(1)}, f32[96,256]{1,0:T(8,128)S(1)}, u32[]{:S(2)}, u32[]{:S(2)}) collective-permute-start(f32[96,256]{1,0:T(8,128)S(1)} %constant_dynamic-slice_fusion.2), channel_id=1, source_target_pairs={{0,4},{1,5},{2,6},{3,7},{4,0},{5,1},{6,2},{7,3},{8,12},{9,13},{10,... | collective-permute-start | bytes 294920 | tf_op jit(solution)/shard_map/ppermute | solution.py:162
  155.5 2.6 %collective-permute-done.10 = f32[96,256]{1,0:T(8,128)S(1)} collective-permute-done((f32[96,256]{1,0:T(8,128)S(1)}, f32[96,256]{1,0:T(8,128)S(1)}, u32[]{:S(2)}, u32[]{:S(2)}) %collective-permute-start.10) | collective-permute-done | bytes 98336 | tf_op jit(solution)/shard_map/ppermute | solution.py:162
  158.2 4.0 %collective-permute-done.11 = f32[48,256]{1,0:T(8,128)S(1)} collective-permute-done((f32[48,256]{1,0:T(8,128)S(1)}, f32[48,256]{1,0:T(8,128)S(1)}, u32[]{:S(2)}, u32[]{:S(2)}) %collective-permute-start.11) | collective-permute-done | bytes 49184 | tf_op jit(solution)/shard_map/ppermute | solution.py:162
  162.3 3.6 %collective-permute-start.12 = (f32[24,256]{1,0:T(8,128)S(1)}, f32[24,256]{1,0:T(8,128)S(1)}, u32[]{:S(2)}, u32[]{:S(2)}) collective-permute-start(f32[24,256]{1,0:T(8,128)S(1)} %constant_dynamic-slice_fusion), channel_id=1, source_target_pairs={{0,16},{1,17},{2,18},{3,19},{4,20},{5,21},{6,22},{7,23},{8,24},{9,... | collective-permute-start | bytes 73736 | tf_op jit(solution)/shard_map/ppermute | solution.py:162
  165.9 2.0 %collective-permute-done.12 = f32[24,256]{1,0:T(8,128)S(1)} collective-permute-done((f32[24,256]{1,0:T(8,128)S(1)}, f32[24,256]{1,0:T(8,128)S(1)}, u32[]{:S(2)}, u32[]{:S(2)}) %collective-permute-start.12) | collective-permute-done | bytes 24608 | tf_op jit(solution)/shard_map/ppermute | solution.py:162
  167.9 2.9 %collective-permute-start.13 = (f32[24,256]{1,0:T(8,128)S(1)}, f32[24,256]{1,0:T(8,128)S(1)}, u32[]{:S(2)}, u32[]{:S(2)}) collective-permute-start(f32[24,256]{1,0:T(8,128)S(1)} %dynamic-slice_add_fusion.4), channel_id=1, source_target_pairs={{0,16},{1,17},{2,18},{3,19},{4,20},{5,21},{6,22},{7,23},{8,24},{9,... | collective-permute-start | bytes 73736 | tf_op jit(solution)/shard_map/ppermute | solution.py:162
  170.7 1.9 collective-permute-done.13
  172.6 2.0 %collective-permute-start.14 = (f32[48,256]{1,0:T(8,128)S(1)}, f32[48,256]{1,0:T(8,128)S(1)}, u32[]{:S(2)}, u32[]{:S(2)}) collective-permute-start(f32[48,256]{1,0:T(8,128)S(1)} %pad_maximum_fusion.5), channel_id=1, source_target_pairs={{0,8},{1,9},{2,10},{3,11},{4,12},{5,13},{6,14},{7,15},{8,0},{9,1},... | collective-permute-start | bytes 147464 | tf_op jit(solution)/shard_map/ppermute | solution.py:162
  174.7 2.1 %collective-permute-done.14 = f32[48,256]{1,0:T(8,128)S(1)} collective-permute-done((f32[48,256]{1,0:T(8,128)S(1)}, f32[48,256]{1,0:T(8,128)S(1)}, u32[]{:S(2)}, u32[]{:S(2)}) %collective-permute-start.14) | collective-permute-done | bytes 49184 | tf_op jit(solution)/shard_map/ppermute | solution.py:162
  176.8 1.8 collective-permute-start.15
  178.6 2.9 %collective-permute-done.15 = f32[96,256]{1,0:T(8,128)S(1)} collective-permute-done((f32[96,256]{1,0:T(8,128)S(1)}, f32[96,256]{1,0:T(8,128)S(1)}, u32[]{:S(2)}, u32[]{:S(2)}) %collective-permute-start.15) | collective-permute-done | bytes 98336 | tf_op jit(solution)/shard_map/ppermute | solution.py:162
  182.0 5.3 %collective-permute-done.16 = f32[192,256]{1,0:T(8,128)S(1)} collective-permute-done((f32[192,256]{1,0:T(8,128)S(1)}, f32[192,256]{1,0:T(8,128)S(1)}, u32[]{:S(2)}, u32[]{:S(2)}) %collective-permute-start.16) | collective-permute-done | bytes 196640 | tf_op jit(solution)/shard_map/ppermute | solution.py:162
  187.5 1.7 collective-permute-done.17
  189.3 1.4 close.1
  (61 shorter events, 2.5 us)
Async XLA Ops:
  6.2 6.8 %copy-start = (bf16[2048,512]{1,0:T(8,128)(2,1)}, bf16[2048,512]{1,0:T(8,128)(2,1)S(1)}, u32[]{:S(2)}) copy-start(bf16[2048,512]{1,0:T(8,128)(2,1)S(1)} %get-tuple-element.14.low_ref) | copy-start | bytes 6291460
  13.0 22.2 %collective-permute-start.5 = (f32[512,512]{1,0:T(8,128)}, f32[512,512]{1,0:T(8,128)}, u32[]{:S(2)}, u32[]{:S(2)}) collective-permute-start(f32[512,512]{1,0:T(8,128)} %product.15), channel_id=1, source_target_pairs={{0,1},{1,0},{2,3},{3,2},{4,5},{5,4},{6,7},{7,6},{8,9},{9,8},{10,11... | collective-permute-start | bytes 3145736 | tf_op jit(solution)/shard_map/ppermute | solution.py:162
  13.5 1.6 copy-start.1
  20.2 43.6 %collective-permute-start.4 = (f32[512,512]{1,0:T(8,128)S(1)}, f32[512,512]{1,0:T(8,128)}, u32[]{:S(2)}, u32[]{:S(2)}) collective-permute-start(f32[512,512]{1,0:T(8,128)S(1)} %product.13), channel_id=1, source_target_pairs={{0,1},{1,0},{2,3},{3,2},{4,5},{5,4},{6,7},{7,6},{8,9},{9,8},{10,11... | collective-permute-start | bytes 3145736 | tf_op jit(solution)/shard_map/ppermute | solution.py:162
  20.4 1.6 copy-start.2
  27.9 32.0 %collective-permute-start.2 = (f32[512,512]{1,0:T(8,128)}, f32[512,512]{1,0:T(8,128)}, u32[]{:S(2)}, u32[]{:S(2)}) collective-permute-start(f32[512,512]{1,0:T(8,128)} %product.11), channel_id=1, source_target_pairs={{0,1},{1,0},{2,3},{3,2},{4,5},{5,4},{6,7},{7,6},{8,9},{9,8},{10,11... | collective-permute-start | bytes 3145736 | tf_op jit(solution)/shard_map/ppermute | solution.py:162
  28.4 1.6 copy-start.3
  37.7 26.2 %collective-permute-start.6 = (f32[512,512]{1,0:T(8,128)}, f32[512,512]{1,0:T(8,128)}, u32[]{:S(2)}, u32[]{:S(2)}) collective-permute-start(f32[512,512]{1,0:T(8,128)} %add.103), channel_id=1, source_target_pairs={{0,2},{1,5},{2,0},{3,7},{4,6},{5,1},{6,4},{7,3},{8,10},{9,13},{10,... | collective-permute-start | bytes 3145736 | tf_op jit(solution)/shard_map/ppermute | solution.py:162
  40.2 1.6 copy-start.4
  47.7 38.5 %collective-permute-start.1 = (f32[512,512]{1,0:T(8,128)}, f32[512,512]{1,0:T(8,128)}, u32[]{:S(2)}, u32[]{:S(2)}) collective-permute-start(f32[512,512]{1,0:T(8,128)} %product.9), channel_id=1, source_target_pairs={{0,1},{1,0},{2,3},{3,2},{4,5},{5,4},{6,7},{7,6},{8,9},{9,8},{10,11... | collective-permute-start | bytes 3145736 | tf_op jit(solution)/shard_map/ppermute | solution.py:162
  48.0 1.6 copy-start.5
  62.4 67.7 %collective-permute-start.3 = (f32[512,512]{1,0:T(8,128)}, f32[512,512]{1,0:T(8,128)}, u32[]{:S(2)}, u32[]{:S(2)}) collective-permute-start(f32[512,512]{1,0:T(8,128)} %add.100), channel_id=1, source_target_pairs={{0,2},{1,5},{2,0},{3,7},{4,6},{5,1},{6,4},{7,3},{8,10},{9,13},{10,... | collective-permute-start | bytes 3145736 | tf_op jit(solution)/shard_map/ppermute | solution.py:162
  66.8 63.3 %collective-permute-start.7 = (f32[512,512]{1,0:T(8,128)}, f32[512,512]{1,0:T(8,128)}, u32[]{:S(2)}, u32[]{:S(2)}) collective-permute-start(f32[512,512]{1,0:T(8,128)} %add_add_fusion), channel_id=1, source_target_pairs={{0,4},{1,3},{2,6},{3,1},{4,0},{5,7},{6,2},{7,5},{8,12},{9,11},{10,... | collective-permute-start | bytes 3145736 | tf_op jit(solution)/shard_map/ppermute | solution.py:162
  67.3 11.8 %copy-start.10 = (s32[64]{0:T(128)S(1)}, s32[64]{0:T(128)}, u32[]{:S(2)}) copy-start(s32[64]{0:T(128)} %param.13) | copy-start | bytes 772
  67.3 11.8 %copy-start.11 = (s32[64]{0:T(128)S(1)}, s32[64]{0:T(128)}, u32[]{:S(2)}) copy-start(s32[64]{0:T(128)} %param.14) | copy-start | bytes 772
  69.6 62.8 %collective-permute-start = (f32[2,512,256]{2,1,0:T(8,128)}, f32[2,512,256]{2,1,0:T(8,128)}, u32[]{:S(2)}, u32[]{:S(2)}) collective-permute-start(f32[2,512,256]{2,1,0:T(8,128)} %pad_maximum_fusion), channel_id=1, source_target_pairs={{0,0},{1,5},{2,10},{3,15},{4,16},{5,21},{6,26},{7,31},{8,1},{9,4},... | collective-permute-start | bytes 3145736 | tf_op jit(solution)/shard_map/ppermute | solution.py:219
  79.4 1.6 copy-start.6
  86.2 46.2 %copy-start.7 = (f32[256,256]{1,0:T(8,128)S(1)}, f32[256,256]{1,0:T(8,128)}, u32[]{:S(2)}) copy-start(f32[256,256]{1,0:T(8,128)} %coupling_ref.3) | copy-start | bytes 786436
  135.1 10.4 %collective-permute-start.8 = (f32[384,256]{1,0:T(8,128)S(1)}, f32[384,256]{1,0:T(8,128)S(1)}, u32[]{:S(2)}, u32[]{:S(2)}) collective-permute-start(f32[384,256]{1,0:T(8,128)S(1)} %constant_dynamic-slice_fusion.4), channel_id=1, source_target_pairs={{0,1},{1,0},{2,3},{3,2},{4,5},{5,4},{6,7},{7,6},{8,9},{9,8},{10,11... | collective-permute-start | bytes 1179656 | tf_op jit(solution)/shard_map/ppermute | solution.py:162
  145.5 7.2 %collective-permute-start.9 = (f32[192,256]{1,0:T(8,128)S(1)}, f32[192,256]{1,0:T(8,128)S(1)}, u32[]{:S(2)}, u32[]{:S(2)}) collective-permute-start(f32[192,256]{1,0:T(8,128)S(1)} %constant_dynamic-slice_fusion.3), channel_id=1, source_target_pairs={{0,2},{1,3},{2,0},{3,1},{4,6},{5,7},{6,4},{7,5},{8,10},{9,11},{10,... | collective-permute-start | bytes 589832 | tf_op jit(solution)/shard_map/ppermute | solution.py:162
  152.8 5.2 %collective-permute-start.10 = (f32[96,256]{1,0:T(8,128)S(1)}, f32[96,256]{1,0:T(8,128)S(1)}, u32[]{:S(2)}, u32[]{:S(2)}) collective-permute-start(f32[96,256]{1,0:T(8,128)S(1)} %constant_dynamic-slice_fusion.2), channel_id=1, source_target_pairs={{0,4},{1,5},{2,6},{3,7},{4,0},{5,1},{6,2},{7,3},{8,12},{9,13},{10,... | collective-permute-start | bytes 294920 | tf_op jit(solution)/shard_map/ppermute | solution.py:162
  158.1 4.2 %collective-permute-start.11 = (f32[48,256]{1,0:T(8,128)S(1)}, f32[48,256]{1,0:T(8,128)S(1)}, u32[]{:S(2)}, u32[]{:S(2)}) collective-permute-start(f32[48,256]{1,0:T(8,128)S(1)} %constant_dynamic-slice_fusion.1), channel_id=1, source_target_pairs={{0,8},{1,9},{2,10},{3,11},{4,12},{5,13},{6,14},{7,15},{8,0},{9,1},... | collective-permute-start | bytes 147464 | tf_op jit(solution)/shard_map/ppermute | solution.py:162
  162.3 5.6 %collective-permute-start.12 = (f32[24,256]{1,0:T(8,128)S(1)}, f32[24,256]{1,0:T(8,128)S(1)}, u32[]{:S(2)}, u32[]{:S(2)}) collective-permute-start(f32[24,256]{1,0:T(8,128)S(1)} %constant_dynamic-slice_fusion), channel_id=1, source_target_pairs={{0,16},{1,17},{2,18},{3,19},{4,20},{5,21},{6,22},{7,23},{8,24},{9,... | collective-permute-start | bytes 73736 | tf_op jit(solution)/shard_map/ppermute | solution.py:162
  167.9 4.7 %collective-permute-start.13 = (f32[24,256]{1,0:T(8,128)S(1)}, f32[24,256]{1,0:T(8,128)S(1)}, u32[]{:S(2)}, u32[]{:S(2)}) collective-permute-start(f32[24,256]{1,0:T(8,128)S(1)} %dynamic-slice_add_fusion.4), channel_id=1, source_target_pairs={{0,16},{1,17},{2,18},{3,19},{4,20},{5,21},{6,22},{7,23},{8,24},{9,... | collective-permute-start | bytes 73736 | tf_op jit(solution)/shard_map/ppermute | solution.py:162
  172.6 4.2 %collective-permute-start.14 = (f32[48,256]{1,0:T(8,128)S(1)}, f32[48,256]{1,0:T(8,128)S(1)}, u32[]{:S(2)}, u32[]{:S(2)}) collective-permute-start(f32[48,256]{1,0:T(8,128)S(1)} %pad_maximum_fusion.5), channel_id=1, source_target_pairs={{0,8},{1,9},{2,10},{3,11},{4,12},{5,13},{6,14},{7,15},{8,0},{9,1},... | collective-permute-start | bytes 147464 | tf_op jit(solution)/shard_map/ppermute | solution.py:162
  176.8 4.7 %collective-permute-start.15 = (f32[96,256]{1,0:T(8,128)S(1)}, f32[96,256]{1,0:T(8,128)S(1)}, u32[]{:S(2)}, u32[]{:S(2)}) collective-permute-start(f32[96,256]{1,0:T(8,128)S(1)} %pad_maximum_fusion.4), channel_id=1, source_target_pairs={{0,4},{1,5},{2,6},{3,7},{4,0},{5,1},{6,2},{7,3},{8,12},{9,13},{10,... | collective-permute-start | bytes 294920 | tf_op jit(solution)/shard_map/ppermute | solution.py:162
  181.5 5.7 %collective-permute-start.16 = (f32[192,256]{1,0:T(8,128)S(1)}, f32[192,256]{1,0:T(8,128)S(1)}, u32[]{:S(2)}, u32[]{:S(2)}) collective-permute-start(f32[192,256]{1,0:T(8,128)S(1)} %pad_maximum_fusion.3), channel_id=1, source_target_pairs={{0,2},{1,3},{2,0},{3,1},{4,6},{5,7},{6,4},{7,5},{8,10},{9,11},{10,... | collective-permute-start | bytes 589832 | tf_op jit(solution)/shard_map/ppermute | solution.py:162
  187.3 2.0 %copy-start.8 = (f32[256,256]{1,0:T(8,128)S(1)}, f32[256,256]{1,0:T(8,128)}, u32[]{:S(2)}) copy-start(f32[256,256]{1,0:T(8,128)} %first_ref.3) | copy-start | bytes 786436
  187.3 2.0 %copy-start.9 = (f32[256,256]{1,0:T(8,128)S(1)}, f32[256,256]{1,0:T(8,128)}, u32[]{:S(2)}) copy-start(f32[256,256]{1,0:T(8,128)} %second_ref.3) | copy-start | bytes 786436
  187.4 1.8 collective-permute-start.17
